TPU v7x, 32 devices: a whole 2x2x4 slice. The times are simulated.
32 devices in a mesh: groups: 2 (over x), fsdp: 16 (over z, y, core).
Axes of the slice: x: 2, y: 2, z: 4, core: 2. Of those that a mesh axis runs over, the one named last changes fastest.
Arguments:
- inputs: bfloat16 [10240, 8192], P(('groups', 'fsdp')), parts along dimension 0, may hold values from -6 to 6
- key_value_gradient: bfloat16 [10240, 2048], P(('groups', 'fsdp')), parts along dimension 0, may hold values from -6 to 6
- kept_frozen_blocks: bfloat16 [2, 320, 128, 128], P(None, 'fsdp'), may hold values from -0.25 to 0.25
- kept: int32 [2, 64, 8], replicated, may hold values from 0 to 1, as said below
- adapter_down_matrices: bfloat16 [16384, 128], P(('groups', 'fsdp')), parts along dimension 0, may hold values from -0.1875 to 0.1875
- adapter_up_matrices: bfloat16 [4, 64, 1024], P('groups'), parts along dimension 0, may hold values from -0.1875 to 0.1875
Outputs:
- grad_inputs: bfloat16 [10240, 8192], P(('groups', 'fsdp')), parts along dimension 0
- grad_down: float32 [16384, 128], P(('groups', 'fsdp')), parts along dimension 0
- grad_up: float32 [4, 64, 1024], P('groups'), parts along dimension 0
There are 2 independent parts, one for each index of `groups`. A program takes and returns all parts, laid end to end along the dimension named above; an argument that names none is the same for every part. Nothing has to cross between parts.
Inputs may be any that keep to these rules, and one draw needn't show every extreme that they name: `kept`: each block-row keeps 3 to 5 blocks; block-rows r and r + 32 of one projection keep 8 blocks together; the block-rows s * 4 to (s + 1) * 4 - 1 keep at most 20 blocks of a projection, and some such set keeps exactly 20.
All inputs are finite; a program needn't handle non-finite values.
Results may differ from a plain program's by a relative error of at most 0.003.
Values may be sent and summed in bfloat16 or wider, within the bound.
A program may use at most 128 MiB of HBM per device.

v0:
```python
import math

import jax
import jax.numpy as jnp
from jax import lax
from jax.sharding import PartitionSpec as P

adapter_scale = 0.5


def token_sum(left_side, right_side):
    return lax.dot_general(
        left_side, right_side, (((0,), (0,)), ((), ())), preferred_element_type=jnp.float32
    )


def project_rows(block_pool, slot_table, keep_table, cotangent):
    row_count = slot_table.shape[1]
    col_blocks = slot_table.shape[2]
    group_rows = math.gcd(row_count, 8)
    block_size = block_pool.shape[-1]
    tokens = cotangent.shape[0]

    def advance(position, result):
        slots_here = lax.dynamic_slice_in_dim(slot_table, position * group_rows, group_rows, 1)
        keep_here = lax.dynamic_slice_in_dim(keep_table, position * group_rows, group_rows, 1)
        taken = jax.vmap(lambda blocks, indices: jnp.take(blocks, indices.reshape(-1), axis=0))(
            block_pool, slots_here
        )
        taken = taken.reshape(2, group_rows, col_blocks, block_size, block_size)
        dense_blocks = jnp.where(
            keep_here[..., None, None] > 0, taken, jnp.zeros((), block_pool.dtype)
        )
        product = jnp.einsum(
            "tmcj,mrcij->tri", cotangent, dense_blocks, preferred_element_type=jnp.float32
        )
        return lax.dynamic_update_slice_in_dim(
            result,
            product.reshape(tokens, group_rows * block_size),
            position * group_rows * block_size,
            1,
        )

    initial = jnp.zeros((tokens, row_count * block_size), jnp.float32)
    return lax.fori_loop(0, row_count // group_rows, advance, initial)


def on_device(
    inputs, key_value_gradient, kept_frozen_blocks, kept, adapter_down_matrices, adapter_up_matrices
):
    shard_count = lax.axis_size("fsdp")
    block_size = kept_frozen_blocks.shape[-1]
    slot_count = kept_frozen_blocks.shape[1]
    row_blocks = kept.shape[1]
    col_blocks = kept.shape[2]
    per_shard = row_blocks // shard_count
    token_row_block = inputs.shape[0]
    low_rank_size = adapter_up_matrices.shape[1]
    key_columns = adapter_up_matrices.shape[2]
    grads_split = key_value_gradient.reshape(token_row_block, 2, col_blocks, block_size)
    key_gradient = key_value_gradient[:, :key_columns]
    value_gradient = key_value_gradient[:, key_columns:]
    down_product_total = lax.all_gather(adapter_down_matrices, "fsdp", axis=0, tiled=True)
    low_rank_product = jnp.concatenate(
        [
            jnp.dot(key_gradient, adapter_up_matrices[0].T, preferred_element_type=jnp.float32),
            jnp.dot(value_gradient, adapter_up_matrices[1].T, preferred_element_type=jnp.float32),
        ],
        axis=1,
    ).astype(jnp.bfloat16)
    hidden_states = jnp.dot(inputs, down_product_total, preferred_element_type=jnp.float32).astype(
        jnp.bfloat16
    )
    adapter_contribution = adapter_scale * jnp.dot(
        low_rank_product, down_product_total.T, preferred_element_type=jnp.float32
    )
    flat_kept = kept.reshape(2, shard_count, per_shard * col_blocks)
    before = (jnp.cumsum(flat_kept, axis=-1) - flat_kept).reshape(2, row_blocks, col_blocks)
    shard_piece = lax.all_gather(kept_frozen_blocks, "fsdp", axis=1, tiled=True)
    covered = shard_piece.shape[1] // slot_count * per_shard
    offsets = (jnp.arange(covered, dtype=jnp.int32) // per_shard * slot_count)[None, :, None]
    slot_table = jnp.where(kept > 0, offsets + before, 0)
    base_term = project_rows(shard_piece, slot_table, kept, grads_split)
    grad_inputs = (base_term + adapter_contribution).astype(jnp.bfloat16)
    gradient_scale = adapter_scale / math.sqrt(token_row_block * shard_count)
    up_partial = gradient_scale * jnp.stack(
        [
            token_sum(hidden_states[:, :low_rank_size], key_gradient),
            token_sum(hidden_states[:, low_rank_size:], value_gradient),
        ]
    )
    grad_down = lax.psum_scatter(
        gradient_scale * token_sum(inputs, low_rank_product),
        "fsdp",
        scatter_dimension=0,
        tiled=True,
    )
    grad_up = lax.psum(up_partial, "fsdp")
    return (grad_inputs, grad_down, grad_up)


def solution(mesh):
    return jax.shard_map(
        on_device,
        mesh=mesh,
        in_specs=(
            P(("groups", "fsdp"), None),
            P(("groups", "fsdp"), None),
            P(None, "fsdp", None, None),
            P(),
            P(("groups", "fsdp"), None),
            P("groups", None, None),
        ),
        out_specs=(
            P(("groups", "fsdp"), None),
            P(("groups", "fsdp"), None),
            P("groups", None, None),
        ),
        check_vma=False,
    )
```

profile of v0, /device:TPU:1, one launch (start us, length us, event | category | flops | bytes accessed | tf_op | source)
XLA Modules:
  0.0 392.6 jit_solution(11317664854143360654)
XLA Ops:
  7.2 0.7 all-gather.5.cloned.1.call-update
  7.9 1.4 convolution_convert_fusion.1
  9.4 1.4 convolution_convert_fusion.2
  11.5 5.8 %fusion.18 = f32[8192,128]{0,1:T(8,128)} fusion(bf16[320,8192]{1,0:T(8,128)(2,1)} %param.8, bf16[320,64]{0,1:T(8,128)(2,1)S(1)} %convolution_convert_fusion.1, bf16[320,64]{0,1:T(8,128)(2,1)S(1)} %convolution_convert_fusion.2), kind=kOutput, calls=%fused_computation.25 | convolution fusion | flops 672301056 | bytes 9519104 | tf_op jit(solution)/shard_map/dot_general | solution.py:12
  19.2 1.4 copy.26
  20.6 0.7 add_select_fusion
  21.3 32.8 %all-gather.5.cloned.1.call-done = bf16[8192,128]{1,0:T(8,128)(2,1)} async-done(((bf16[512,128]{1,0:T(8,128)(2,1)}), bf16[8192,128]{1,0:T(8,128)(2,1)}) %all-gather.5.cloned.1.call-update) | async-done | bytes 2097168 | tf_op jit(solution)/shard_map/all_gather | solution.py:63
  54.1 4.7 %convolution_convert_fusion = bf16[320,128]{1,0:T(8,128)(2,1)S(1)} fusion(bf16[320,8192]{1,0:T(8,128)(2,1)} %param.8, bf16[8192,128]{1,0:T(8,128)(2,1)} %all-gather.5.cloned.1.call-done), kind=kOutput, calls=%fused_computation.28 | convolution fusion | flops 671129600 | bytes 7421952 | tf_op jit(solution)/shard_map/dot_general | solution.py:71
  59.4 0.8 maximum_multiply_fusion
  60.3 67.3 %reduce-scatter.2.cloned.1.call-done = f32[512,128]{0,1:T(8,128)} async-done(((f32[8192,128]{0,1:T(8,128)}), f32[512,128]{0,1:T(8,128)}) %reduce-scatter.2.cloned.1.call-update) | async-done | bytes 262160 | tf_op jit(solution)/shard_map/reduce_scatter | solution.py:92
  127.6 1.8 copy.27
  129.4 109.9 %all-gather.3.cloned.1.call-done = bf16[2,320,128,128]{3,2,1,0:T(8,128)(2,1)} async-done(((bf16[2,20,128,128]{3,2,1,0:T(8,128)(2,1)}), bf16[2,320,128,128]{3,2,1,0:T(8,128)(2,1)}) %all-gather.3.cloned.1.call-update) | async-done | bytes 20971536 | tf_op jit(solution)/shard_map/all_gather | solution.py:79
  239.3 5.2 %broadcast_in_dim.55 = f32[320,8192]{1,0:T(8,128)} broadcast(f32[]{:T(128)} %constant.134.clone.1), dimensions={} | broadcast | bytes 10485764 | tf_op jit(solution)/shard_map/broadcast_in_dim | solution.py:44
  244.5 131.8 %while.15 = (s32[]{:T(128)}, f32[320,8192]{1,0:T(8,128)}, s32[2,64,8]{2,1,0:T(8,128)S(1)}, s32[2,64,8]{2,1,0:T(8,128)}, bf16[2,320,128,128]{3,2,1,0:T(8,128)(2,1...) while((s32[]{:T(128)}, f32[320,8192]{1,0:T(8,128)}, ...), condition=%wide.region_2.3_spmd, body=%wide.region_1.2_spmd.sunk | while | flops 1346373504 | bytes 17832664 | solution.py:45
  244.5 0.9 compare_and_fusion.2
  245.5 10.2 %gather_fusion = bf16[128,128,128]{2,1,0:T(8,128)(2,1)} fusion(bf16[2,320,128,128]{3,2,1,0:T(8,128)(2,1)} %get-tuple-element.262, s32[128]{0:T(128)S(1)} %reshape.122), kind=kCustom, calls=%fused_computation.clone.1 | custom fusion | bytes 8389632 | tf_op jit(solution)/shard_map/while/body/eval_jaxpr/vmap(jit(_take))/gather | solution.py:27
  256.0 3.9 fusion.43
  259.9 1.2 bitcast_dynamic-update-slice_fusion.2
  261.1 0.7 compare_and_fusion.2
  262.0 10.2 %gather_fusion = bf16[128,128,128]{2,1,0:T(8,128)(2,1)} fusion(bf16[2,320,128,128]{3,2,1,0:T(8,128)(2,1)} %get-tuple-element.262, s32[128]{0:T(128)S(1)} %reshape.122), kind=kCustom, calls=%fused_computation.clone.1 | custom fusion | bytes 8389632 | tf_op jit(solution)/shard_map/while/body/eval_jaxpr/vmap(jit(_take))/gather | solution.py:27
  272.4 3.9 fusion.43
  276.4 1.3 bitcast_dynamic-update-slice_fusion.2
  277.6 0.7 compare_and_fusion.2
  278.5 10.2 %gather_fusion = bf16[128,128,128]{2,1,0:T(8,128)(2,1)} fusion(bf16[2,320,128,128]{3,2,1,0:T(8,128)(2,1)} %get-tuple-element.262, s32[128]{0:T(128)S(1)} %reshape.122), kind=kCustom, calls=%fused_computation.clone.1 | custom fusion | bytes 8389632 | tf_op jit(solution)/shard_map/while/body/eval_jaxpr/vmap(jit(_take))/gather | solution.py:27
  289.0 3.9 fusion.43
  292.9 1.2 bitcast_dynamic-update-slice_fusion.2
  294.1 0.7 compare_and_fusion.2
  295.0 10.1 %gather_fusion = bf16[128,128,128]{2,1,0:T(8,128)(2,1)} fusion(bf16[2,320,128,128]{3,2,1,0:T(8,128)(2,1)} %get-tuple-element.262, s32[128]{0:T(128)S(1)} %reshape.122), kind=kCustom, calls=%fused_computation.clone.1 | custom fusion | bytes 8389632 | tf_op jit(solution)/shard_map/while/body/eval_jaxpr/vmap(jit(_take))/gather | solution.py:27
  305.4 3.9 fusion.43
  309.3 1.3 bitcast_dynamic-update-slice_fusion.2
  310.6 0.7 compare_and_fusion.2
  311.5 10.2 %gather_fusion = bf16[128,128,128]{2,1,0:T(8,128)(2,1)} fusion(bf16[2,320,128,128]{3,2,1,0:T(8,128)(2,1)} %get-tuple-element.262, s32[128]{0:T(128)S(1)} %reshape.122), kind=kCustom, calls=%fused_computation.clone.1 | custom fusion | bytes 8389632 | tf_op jit(solution)/shard_map/while/body/eval_jaxpr/vmap(jit(_take))/gather | solution.py:27
  321.9 3.9 fusion.43
  325.8 1.2 bitcast_dynamic-update-slice_fusion.2
  327.0 0.7 compare_and_fusion.2
  327.9 10.1 %gather_fusion = bf16[128,128,128]{2,1,0:T(8,128)(2,1)} fusion(bf16[2,320,128,128]{3,2,1,0:T(8,128)(2,1)} %get-tuple-element.262, s32[128]{0:T(128)S(1)} %reshape.122), kind=kCustom, calls=%fused_computation.clone.1 | custom fusion | bytes 8389632 | tf_op jit(solution)/shard_map/while/body/eval_jaxpr/vmap(jit(_take))/gather | solution.py:27
  338.3 3.9 fusion.43
  342.2 1.2 bitcast_dynamic-update-slice_fusion.2
  343.5 0.7 compare_and_fusion.2
  344.4 10.1 %gather_fusion = bf16[128,128,128]{2,1,0:T(8,128)(2,1)} fusion(bf16[2,320,128,128]{3,2,1,0:T(8,128)(2,1)} %get-tuple-element.262, s32[128]{0:T(128)S(1)} %reshape.122), kind=kCustom, calls=%fused_computation.clone.1 | custom fusion | bytes 8389632 | tf_op jit(solution)/shard_map/while/body/eval_jaxpr/vmap(jit(_take))/gather | solution.py:27
  354.7 3.9 fusion.43
  358.6 1.2 bitcast_dynamic-update-slice_fusion.2
  359.9 0.7 compare_and_fusion.2
  360.7 10.1 %gather_fusion = bf16[128,128,128]{2,1,0:T(8,128)(2,1)} fusion(bf16[2,320,128,128]{3,2,1,0:T(8,128)(2,1)} %get-tuple-element.262, s32[128]{0:T(128)S(1)} %reshape.122), kind=kCustom, calls=%fused_computation.clone.1 | custom fusion | bytes 8389632 | tf_op jit(solution)/shard_map/while/body/eval_jaxpr/vmap(jit(_take))/gather | solution.py:27
  371.1 3.9 fusion.43
  375.0 1.2 bitcast_dynamic-update-slice_fusion.2
  376.3 7.9 %fusion.17 = bf16[320,8192]{1,0:T(8,128)(2,1)} fusion(f32[320,8192]{1,0:T(8,128)} %get-tuple-element.157, bf16[8192,128]{1,0:T(8,128)(2,1)S(1)} %copy-done, bf16[320,64]{0,1:T(8,128)(2,1)S(1)} %convolution_convert_fusion.1, bf16[320,64]{0,1:T(8,128)(2,1)} %copy-done.2), kind=kOutput, calls=%fused_computation.23 | convolution fusion | flops 679116800 | bytes 17907712 | tf_op jit(solution)/shard_map/dot_general | solution.py:74
  384.2 1.9 copy.58
  (66 shorter events, 6.8 us)
Async XLA Ops:
  7.2 46.9 %all-gather.5.cloned.1.call-start = ((), (), s32[]{:S(2)}) async-start(), calls=%async_computation.2 | async-start | bytes 2228224 | tf_op jit(solution)/shard_map/all_gather | solution.py:63
  7.9 119.7 %reduce-scatter.2.cloned.1.call-start = ((), (), s32[]{:S(2)}) async-start(), calls=%async_computation.3 | async-start | bytes 4456448 | tf_op jit(solution)/shard_map/reduce_scatter | solution.py:92
  10.9 0.6 copy-start.2
  17.2 0.8 copy-start.3
  17.2 1.6 copy-start.1
  17.3 222.0 %all-gather.3.cloned.1.call-start = ((), (), s32[]{:S(2)}) async-start(), calls=%async_computation.1 | async-start | bytes 22282240 | tf_op jit(solution)/shard_map/all_gather | solution.py:79
  18.0 366.2 %all-reduce.2.cloned.1.call-start = ((), (), s32[]{:S(2)}) async-start(), calls=%async_computation.4 | async-start | bytes 1048576 | tf_op jit(solution)/shard_map/psum | solution.py:98
  244.5 131.8 %copy-start = (bf16[8192,128]{1,0:T(8,128)(2,1)S(1)}, bf16[8192,128]{1,0:T(8,128)(2,1)}, u32[]{:S(2)}) copy-start(bf16[8192,128]{1,0:T(8,128)(2,1)} %all-gather.5.cloned.1.call-done) | copy-start | bytes 6291460
Sparse Core Ops, SparseCore 0:
  10.2 43.8 all-gather.4
  58.5 69.0 reduce-scatter.1
  129.2 109.9 all-gather.2
  243.5 90.3 all-reduce.1
where the time goes:
time: 394 us; the launch traced here: 393 us
  waiting for transfers between devices  211 us (54%)
  local copies, waits for them, and re-layouts  106 us (27%)
  matrix products  53.2 us (14%)
  between operations  13.9 us (4%)
  other arithmetic  7.84 us (2%)
    all_gather x1, waiting for transfers between devices, on_device(): shard_piece = lax.all_gather(kept_frozen_blocks, 'fsdp', axis=1, tiled=True)  110 us
    gather x16, local copies, waits for them, and re-layouts, advance(): jnp.take(blocks, indices.reshape(-1), axis=0)  81.8 us
    reduce_scatter x1, waiting for transfers between devices, on_device(): lax.psum_scatter(gradient_scale * token_sum(inputs, low_rank_product), 'f...  67.3 us
    all_gather x1, waiting for transfers between devices, on_device(): lax.all_gather(adapter_down_matrices, 'fsdp', axis=0, tiled=True)  32.8 us
    dot_general x8, matrix products, advance(): jnp.einsum('tmcj,mrcij->tri', cotangent, dense_blocks, preferred_element_...  31.2 us
    dynamic_update_slice x8, local copies, waits for them, and re-layouts, advance(): lax.dynamic_update_slice_in_dim(result, product.reshape(tokens, group_row...  9.85 us
    dot_general x1, matrix products, on_device(): jnp.dot(low_rank_product, down_product_total.T, preferred_element_type=jn...  7.93 us
  transfers between devices with their start and end apart: 4, of which 3 were waited for; matrix products, arithmetic and copies ran while one was open for 42% of the time, Pallas kernels for 0%

commit v1 on v0

v1 whole, which is shorter than its diff:
```python
import functools
import math

import jax
import jax.numpy as jnp
from jax import lax
from jax.experimental import pallas as pl
from jax.experimental.pallas import tpu as pltpu
from jax.sharding import PartitionSpec as P

adapter_scale = 0.5
F32 = jnp.float32
BF16 = jnp.bfloat16


def dot(a, b, ca, cb):
    return lax.dot_general(a, b, (((ca,), (cb,)), ((), ())), preferred_element_type=F32)


def exchange_kernel(
    n,
    scale,
    count_ref,
    x_ref,
    g_ref,
    kfb_ref,
    a_ref,
    b_ref,
    wbuf,
    abuf,
    low_ref,
    down_ref,
    ubuf,
    wown,
    ovf,
    parts,
    rc,
    ry,
    rz,
    uparts,
    uc,
    uy,
    uz,
    asem,
    wsem_z,
    wsem_y,
    wsem_x,
    wsem_c,
    osem,
    dsem,
    dzsem,
    usem,
    uzsem,
    gsem,
    lsem,
):
    zs = n // 4
    group = lax.axis_index("groups")
    me = lax.axis_index("fsdp")
    k = lax.rem(me, 2)
    y = lax.rem(me // 2, 2)
    z = me // 4
    m = lax.rem(group, 2)
    other_group = group + 1 - 2 * m

    def place(dz, dy, dk):
        zz = lax.rem(z + dz, zs)
        yy = y if dy == 0 else 1 - y
        kk = k if dk == 0 else 1 - k
        return (zz * 2 + yy) * 2 + kk

    def device(dz=0, dy=0, dk=0, dx=0):
        return (group if dx == 0 else other_group, place(dz % zs, dy, dk))

    sends = []

    def send(src, dst, ssem, rsem, target):
        copy = pltpu.make_async_remote_copy(
            src_ref=src,
            dst_ref=dst,
            send_sem=ssem,
            recv_sem=rsem,
            device_id=target,
            device_id_type=pl.DeviceIdType.MESH,
        )
        copy.start()
        sends.append(copy)

    def arrived(ref, ssem, rsem, source):
        pltpu.make_async_remote_copy(
            src_ref=ref,
            dst_ref=ref,
            send_sem=ssem,
            recv_sem=rsem,
            device_id=source,
            device_id_type=pl.DeviceIdType.MESH,
        ).wait_recv()

    sibling = device(dk=1)
    across_y = device(dy=1)
    across_x = device(dx=1)
    partners = [sibling, across_y, across_x] + [device(dz=dz) for dz in range(1, zs)]
    barrier = pltpu.get_barrier_semaphore()
    for partner in partners:
        pl.semaphore_signal(
            barrier, inc=1, device_id=partner, device_id_type=pl.DeviceIdType.MESH
        )
    pl.semaphore_wait(barrier, len(partners))

    def gather_start(buf, sem):
        own = buf.at[me]
        for dz in range(1, zs):
            send(own, own, sem.at[0, 0, dz], sem.at[0, 1, dz], device(dz=-dz))
        send(own, own, sem.at[1, 0, 0], sem.at[1, 1, 0], across_y)
        send(own, own, sem.at[2, 0, 0], sem.at[2, 1, 0], sibling)

    def gather_middle(buf, sem):
        for dz in range(1, zs):
            piece = buf.at[place(dz, 0, 0)]
            arrived(piece, sem.at[0, 0, dz], sem.at[0, 1, dz], device(dz=dz))
            send(piece, piece, sem.at[1, 0, dz], sem.at[1, 1, dz], across_y)
            send(piece, piece, sem.at[2, 0, dz], sem.at[2, 1, dz], sibling)
        for dz in range(zs):
            piece = buf.at[place(dz, 1, 0)]
            arrived(piece, sem.at[1, 0, dz], sem.at[1, 1, dz], across_y)
            send(piece, piece, sem.at[2, 0, zs + dz], sem.at[2, 1, zs + dz], sibling)

    def gather_end(buf, sem):
        for dz in range(zs):
            for dy in range(2):
                slot = dy * zs + dz
                arrived(
                    buf.at[place(dz, dy, 1)], sem.at[2, 0, slot], sem.at[2, 1, slot], sibling
                )

    slots = kfb_ref.shape[1]
    per_shard = slots // 5
    full = 4 * per_shard
    least = 3 * per_shard

    send(kfb_ref.at[:, pl.ds(full, per_shard)], ovf, osem.at[0], osem.at[1], device(dz=zs // 2))
    abuf[me] = a_ref[...]
    gather_start(abuf, asem)

    wown[:, 0:least] = kfb_ref[:, 0:least]
    rank = b_ref.shape[1]
    width = b_ref.shape[2]
    lows = [dot(g_ref[:, p * width : (p + 1) * width], b_ref[p], 1, 1) for p in range(2)]
    low_ref[...] = jnp.concatenate(lows, axis=1).astype(BF16)

    arrived(ovf, osem.at[0], osem.at[1], device(dz=zs // 2))
    for p in range(2):
        held = count_ref[p]
        for t in range(per_shard):
            slot = least + t
            extra = ovf[p, jnp.clip(slot - held, 0, per_shard - 1)]
            wown[p, slot] = jnp.where(slot < held, kfb_ref[p, slot], extra)

    mine = wown.at[m]
    for dz in range(1, zs):
        send(mine, wbuf.at[m, me], wsem_z.at[0, dz], wsem_z.at[1, dz], device(dz=-dz))
    send(mine, wbuf.at[m, me], wsem_y.at[0, 0], wsem_y.at[1, 0], across_y)
    send(mine, wbuf.at[m, me], wsem_c.at[0, 0, 0], wsem_c.at[1, 0, 0], sibling)
    send(wown.at[1 - m], wbuf.at[1 - m, me], wsem_c.at[0, 1, 0], wsem_c.at[1, 1, 0], sibling)
    keep_own = pltpu.make_async_copy(wown, wbuf.at[:, me], lsem)
    keep_own.start()

    low_t = low_ref[...].astype(F32).T.astype(BF16)
    cols = a_ref.shape[0]

    def down_parts(dk):
        kk = k if dk == 0 else 1 - k
        for yy in range(2):

            def body(zz, carry):
                owner = (zz * 2 + yy) * 2 + kk
                at = pl.ds(pl.multiple_of(owner * cols, cols), cols)
                parts[dk, yy, zz] = scale * dot(low_t, x_ref[:, at], 1, 0)
                return carry

            lax.fori_loop(0, zs, body, 0)

    down_parts(1)
    send(parts.at[1], rc, dsem.at[0, 0], dsem.at[0, 1], sibling)
    down_parts(0)

    def w_from_z(dz):
        piece = wbuf.at[m, place(dz, 0, 0)]
        arrived(piece, wsem_z.at[0, dz], wsem_z.at[1, dz], device(dz=dz))
        send(piece, piece, wsem_y.at[0, dz], wsem_y.at[1, dz], across_y)
        send(piece, piece, wsem_x.at[0, dz], wsem_x.at[1, dz], across_x)
        send(piece, piece, wsem_c.at[0, 0, dz], wsem_c.at[1, 0, dz], sibling)

    def w_from_y(dz):
        slot = zs + dz
        piece = wbuf.at[m, place(dz, 1, 0)]
        arrived(piece, wsem_y.at[0, dz], wsem_y.at[1, dz], across_y)
        send(piece, piece, wsem_x.at[0, slot], wsem_x.at[1, slot], across_x)
        send(piece, piece, wsem_c.at[0, 0, slot], wsem_c.at[1, 0, slot], sibling)

    def w_from_x(dz, dy):
        slot = dy * zs + dz
        piece = wbuf.at[1 - m, place(dz, dy, 0)]
        arrived(piece, wsem_x.at[0, slot], wsem_x.at[1, slot], across_x)
        send(piece, piece, wsem_c.at[0, 1, slot], wsem_c.at[1, 1, slot], sibling)

    def reduce_y(own, received, landing, ssem, rsem):
        own[0, 1 - y] = own[0, 1 - y] + received[1 - y]
        send(own.at[0, 1 - y], landing, ssem, rsem, across_y)
        own[0, y] = own[0, y] + received[y]

    def reduce_z(own, received, landing, sem):
        own[0, y] = own[0, y] + received[...]
        for dz in range(1, zs):
            send(
                own.at[0, y, lax.rem(z + zs - dz, zs)],
                landing.at[dz],
                sem.at[0, dz],
                sem.at[1, dz],
                device(dz=-dz),
            )

    def reduce_end(own, landing, sem):
        total = own[0, y, z]
        for dz in range(1, zs):
            arrived(landing.at[dz], sem.at[0, dz], sem.at[1, dz], device(dz=dz))
            total = total + landing[dz]
        return total

    gather_middle(abuf, asem)
    arrived(rc, dsem.at[0, 0], dsem.at[0, 1], sibling)
    reduce_y(parts, rc, ry, dsem.at[1, 0], dsem.at[1, 1])
    w_from_z(1)
    w_from_y(0)
    arrived(ry, dsem.at[1, 0], dsem.at[1, 1], across_y)
    reduce_z(parts, ry, rz, dzsem)
    gather_end(abuf, asem)

    hidden = jnp.zeros((x_ref.shape[0], 2 * rank), F32)

    def hidden_step(owner, total):
        at = pl.ds(pl.multiple_of(owner * cols, cols), cols)
        return total + dot(x_ref[:, at], abuf[owner], 1, 0)

    hidden = lax.fori_loop(0, n, hidden_step, hidden).astype(BF16)
    rows = 2 * rank // n
    hidden_t = hidden.astype(F32).T.astype(BF16)
    ups = scale * jnp.concatenate(
        [
            dot(hidden_t[p * rank : (p + 1) * rank], g_ref[:, p * width : (p + 1) * width], 1, 0)
            for p in range(2)
        ],
        axis=0,
    )
    for owner in range(n):
        kk, yy, zz = owner % 2, owner // 2 % 2, owner // 4
        dk = lax.rem(k + kk, 2)
        uparts[dk, yy, zz] = ups[owner * rows : (owner + 1) * rows]
    send(uparts.at[1], uc, usem.at[0, 0], usem.at[0, 1], sibling)

    for dz in range(2, zs):
        w_from_z(dz)
        w_from_y(dz - 1)
        if dz == 2:
            arrived(uc, usem.at[0, 0], usem.at[0, 1], sibling)
            reduce_y(uparts, uc, uy, usem.at[1, 0], usem.at[1, 1])
    arrived(uy, usem.at[1, 0], usem.at[1, 1], across_y)
    reduce_z(uparts, uy, uz, uzsem)
    w_from_x(1, 0)
    w_from_x(0, 1)
    down_ref[...] = reduce_end(parts, rz, dzsem)
    w_from_y(zs - 1)
    ubuf[me] = reduce_end(uparts, uz, uzsem)
    gather_start(ubuf, gsem)
    for dz in range(2, zs):
        w_from_x(dz, 0)
        w_from_x(dz - 1, 1)
        if dz == 2:
            gather_middle(ubuf, gsem)
    w_from_x(zs - 1, 1)
    gather_end(ubuf, gsem)
    for p in range(2):
        at = m if p == 0 else 1 - m
        for dz in range(zs):
            for dy in range(2):
                slot = dy * zs + dz
                arrived(
                    wbuf.at[at, place(dz, dy, 1)],
                    wsem_c.at[0, p, slot],
                    wsem_c.at[1, p, slot],
                    sibling,
                )
    for copy in sends:
        copy.wait_send()
    keep_own.wait()


def rows_kernel(row_blocks, table_ref, w_ref, a_ref, g_ref, low_ref, out_ref, dense):
    shard = pl.program_id(1) * pl.num_programs(0) + pl.program_id(0)
    full = w_ref.shape[3]
    block = w_ref.shape[-1]
    per_shard = out_ref.shape[1] // block
    col_blocks = g_ref.shape[1] // (2 * block)
    zero = jnp.zeros((block, block), BF16)
    for m in range(2):
        for r in range(per_shard):
            for c in range(col_blocks):
                code = table_ref[(m * row_blocks + shard * per_shard + r) * col_blocks + c]
                at = jnp.maximum(code, 0)
                taken = w_ref[m, at // full, 0, lax.rem(at, full)]
                col = (m * col_blocks + c) * block
                dense[r * block : (r + 1) * block, col : col + block] = jnp.where(
                    code >= 0, taken, zero
                )
    total = dot(g_ref[...], dense[...], 1, 1)
    total = total + adapter_scale * dot(low_ref[...], a_ref[...], 1, 1)
    out_ref[...] = total.astype(BF16)


def on_device(
    inputs, key_value_gradient, kept_frozen_blocks, kept, adapter_down_matrices, adapter_up_matrices
):
    n = lax.axis_size("fsdp")
    zs = n // 4
    tokens, model_width = inputs.shape
    slot_count = kept_frozen_blocks.shape[1]
    block = kept_frozen_blocks.shape[-1]
    row_blocks, col_blocks = kept.shape[1:]
    per_shard = row_blocks // n
    full = 4 * per_shard
    rank, width = adapter_up_matrices.shape[1:]
    cols = adapter_down_matrices.shape[0]
    rows = 2 * rank // n
    scale = adapter_scale / math.sqrt(tokens * n)

    flat = kept.reshape(2, n, per_shard * col_blocks)
    before = jnp.cumsum(flat, axis=-1) - flat
    counts = flat.sum(axis=-1)
    half = (jnp.arange(n, dtype=jnp.int32) // (n // 2))[None, :, None]
    code = jnp.where(
        before < full,
        half * full + before,
        (1 - half) * full + (2 * full - counts[:, :, None]) + before - full,
    )
    table = jnp.where(flat > 0, code, -1).reshape(-1).astype(jnp.int32)
    own_counts = lax.dynamic_index_in_dim(counts, lax.axis_index("fsdp"), 1, keepdims=False)

    vmem = pl.BlockSpec(memory_space=pltpu.VMEM)
    smem = pl.BlockSpec(memory_space=pltpu.SMEM)
    hbm = pl.BlockSpec(memory_space=pl.ANY)
    dma = pltpu.SemaphoreType.DMA
    wbuf, abuf, low, down_t, ubuf = pl.pallas_call(
        functools.partial(exchange_kernel, n, scale),
        out_shape=(
            jax.ShapeDtypeStruct((2, n, full, block, block), BF16),
            jax.ShapeDtypeStruct((n, cols, 2 * rank), BF16),
            jax.ShapeDtypeStruct((tokens, 2 * rank), BF16),
            jax.ShapeDtypeStruct((2 * rank, cols), F32),
            jax.ShapeDtypeStruct((n, rows, width), F32),
        ),
        in_specs=[smem, vmem, vmem, vmem, vmem, vmem],
        out_specs=(hbm, vmem, vmem, vmem, vmem),
        scratch_shapes=[
            pltpu.VMEM((2, full, block, block), BF16),
            pltpu.VMEM((2, per_shard, block, block), BF16),
            pltpu.VMEM((2, 2, zs, 2 * rank, cols), F32),
            pltpu.VMEM((2, zs, 2 * rank, cols), F32),
            pltpu.VMEM((zs, 2 * rank, cols), F32),
            pltpu.VMEM((zs, 2 * rank, cols), F32),
            pltpu.VMEM((2, 2, zs, rows, width), F32),
            pltpu.VMEM((2, zs, rows, width), F32),
            pltpu.VMEM((zs, rows, width), F32),
            pltpu.VMEM((zs, rows, width), F32),
            dma((3, 2, 2 * zs)),
            dma((2, zs)),
            dma((2, zs)),
            dma((2, 2 * zs)),
            dma((2, 2, 2 * zs)),
            dma((2,)),
            dma((2, 2)),
            dma((2, zs)),
            dma((2, 2)),
            dma((2, zs)),
            dma((3, 2, 2 * zs)),
            dma(()),
        ],
        compiler_params=pltpu.CompilerParams(
            collective_id=0, has_side_effects=True, vmem_limit_bytes=48 * 2**20
        ),
        name="exchange",
    )(
        own_counts,
        inputs,
        key_value_gradient,
        kept_frozen_blocks,
        adapter_down_matrices,
        adapter_up_matrices,
    )

    shard_cols = per_shard * block
    grad_inputs = pl.pallas_call(
        functools.partial(rows_kernel, row_blocks),
        out_shape=jax.ShapeDtypeStruct((tokens, model_width), BF16),
        grid_spec=pltpu.PrefetchScalarGridSpec(
            num_scalar_prefetch=1,
            grid=(n // 2, 2),
            in_specs=[
                pl.BlockSpec(
                    (2, 2, 1, full, block, block), lambda p, h, t: (0, 0, p, 0, 0, 0)
                ),
                pl.BlockSpec((shard_cols, 2 * rank), lambda p, h, t: (h * (n // 2) + p, 0)),
                pl.BlockSpec((tokens, 2 * width), lambda p, h, t: (0, 0)),
                pl.BlockSpec((tokens, 2 * rank), lambda p, h, t: (0, 0)),
            ],
            out_specs=pl.BlockSpec((tokens, shard_cols), lambda p, h, t: (0, h * (n // 2) + p)),
            scratch_shapes=[pltpu.VMEM((shard_cols, 2 * width), BF16)],
        ),
        compiler_params=pltpu.CompilerParams(vmem_limit_bytes=40 * 2**20),
        name="rows",
    )(
        table,
        wbuf.reshape(2, 2, n // 2, full, block, block),
        abuf.reshape(n * cols, 2 * rank),
        key_value_gradient,
        low,
    )
    return grad_inputs, down_t.T, ubuf.reshape(2, rank, width)


def solution(mesh):
    return jax.shard_map(
        on_device,
        mesh=mesh,
        in_specs=(
            P(("groups", "fsdp"), None),
            P(("groups", "fsdp"), None),
            P(None, "fsdp", None, None),
            P(),
            P(("groups", "fsdp"), None),
            P("groups", None, None),
        ),
        out_specs=(
            P(("groups", "fsdp"), None),
            P(("groups", "fsdp"), None),
            P("groups", None, None),
        ),
        check_vma=False,
    )
```

time: 394 us -> 183 us (0.46)
  the two profiles are of different devices: /device:TPU:1 before, /device:TPU:13 now
where the time goes in v1:
time: 183 us
  Pallas kernels  173 us (95%)
  local copies, waits for them, and re-layouts  7.71 us (4%)
    pallas_call x1, Pallas kernels, on_device(): pl.pallas_call(functools.partial(exchange_kernel, n, scale), out_shape=(j...  148 us
    pallas_call x1, Pallas kernels, on_device(): pl.pallas_call(functools.partial(rows_kernel, row_blocks), out_shape=jax....  25.4 us
    unnamed x11, local copies, waits for them, and re-layouts  6.91 us

profile of v1, /device:TPU:13, one launch (start us, length us, event | category | flops | bytes accessed | tf_op | source)
XLA Modules:
  0.0 182.7 jit_solution(3744221610212786959)
XLA Ops:
  0.7 0.7 reduce_sum.10
  1.4 0.1 reduce_sum.14
  1.5 0.1 reduce_sum.18
  1.6 0.2 dynamic-slice_reduce_fusion.count_ref
  1.8 0.1 add.54
  1.8 0.1 add.55
  1.9 0.1 add.49
  2.0 0.1 add.50
  2.1 0.8 copy.18
  2.9 0.1 reshape.67
  3.0 0.1 reshape.68
  3.0 0.4 reduce_window_sum.13
  3.4 0.1 reduce_window_sum.14
  3.5 0.0 copy-start
  3.5 1.3 copy-done
  4.8 0.0 copy-start.1
  4.8 1.3 copy-done.1
  6.2 0.0 copy-start.2
  6.2 0.9 copy-done.2
  7.1 0.0 copy-start.3
  7.1 0.9 copy-done.3
  8.0 147.7 %exchange.1 = (bf16[2,16,16,128,128]{4,3,2,1,0:T(8,128)(2,1)}, bf16[16,512,128]{2,1,0:T(8,128)(2,1)S(1)}, bf16[320,128]{1,0:T(8,128)(2,1)S(1)}, f32[128,512]{1,0:T(8,128)S(1)}, f32[16,8,1024]{2,1,0:T(8,128)S(1)}) custom-call(s32[2]{0:T(128)S(1)} %dynamic-slice_reduce_fusion.count_ref, bf16[320,8192]{1,0:T(8,128)(2,1)} %x_ref.1, ...), custom_call_target="tpu_custom_call" | custom-call | tf_op jit(solution)/shard_map/exchange/pallas_call | solution.py:352
  155.7 25.4 %rows.1 = bf16[320,8192]{1,0:T(8,128)(2,1)} custom-call(s32[1024]{0:T(1024)S(1)} %select_select_fusion.table_ref, bf16[2,2,8,16,128,128]{5,4,3,2,1,0:T(8,128)(2,1)} %bitcast.7, bf16[8192,128]{1,0:T(8,128)(2,1)S(1)} %bitcast.4, bf16[320,2048]{1,0:T(8,128)(2,1)S(1)} %copy-done, bf16[320,128]{1,0:T(8,128)(2,1)S(1)} %get-tuple-element.10.low_ref), custom_call_target="tpu_custom_call" | custom-call | tf_op jit(solution)/shard_map/rows/pallas_call | solution.py:401
  181.1 0.8 copy.20
  182.0 0.8 copy.22
  (4 shorter events, 0.0 us)
Async XLA Ops:
  3.5 1.3 copy-start
  4.8 1.3 copy-start.1
  6.2 0.9 copy-start.2
  7.1 0.9 copy-start.3

commit v2 on v1

--- a/solution.py
+++ b/solution.py
@@ -74,7 +74,7 @@
 
     sends = []
 
-    def send(src, dst, ssem, rsem, target):
+    def send(src, dst, ssem, rsem, target, when=None):
         copy = pltpu.make_async_remote_copy(
             src_ref=src,
             dst_ref=dst,
@@ -83,8 +83,11 @@
             device_id=target,
             device_id_type=pl.DeviceIdType.MESH,
         )
-        copy.start()
-        sends.append(copy)
+        if when is None:
+            copy.start()
+        else:
+            pl.when(when)(copy.start)
+        sends.append((copy, when))
 
     def arrived(ref, ssem, rsem, source):
         pltpu.make_async_remote_copy(
@@ -142,7 +145,48 @@
     abuf[me] = a_ref[...]
     gather_start(abuf, asem)
 
-    wown[:, 0:least] = kfb_ref[:, 0:least]
+    half = full // 2
+
+    def chunk(p, owner, c):
+        return wbuf.at[p, owner, pl.ds(c * half, half)]
+
+    def w_start(own, c):
+        mine = own.at[m, pl.ds(0, half)]
+        to = chunk(m, me, c)
+        send(
+            mine,
+            to,
+            wsem_z.at[0, c, 0, 1],
+            wsem_z.at[1, c, 0, 1],
+            device(dz=-1),
+            z > 0,
+        )
+        send(
+            mine,
+            to,
+            wsem_z.at[0, c, 0, zs - 1],
+            wsem_z.at[1, c, 0, zs - 1],
+            device(dz=1),
+            z < zs - 1,
+        )
+        send(mine, to, wsem_y.at[0, c, 0], wsem_y.at[1, c, 0], across_y)
+        for p in range(2):
+            at = m if p == 0 else 1 - m
+            send(
+                own.at[at, pl.ds(0, half)],
+                chunk(at, me, c),
+                wsem_c.at[0, p, c, 0],
+                wsem_c.at[1, p, c, 0],
+                sibling,
+            )
+
+    w_start(kfb_ref, 0)
+    keep_first = pltpu.make_async_copy(
+        kfb_ref.at[:, pl.ds(0, half)], wbuf.at[:, me, pl.ds(0, half)], lsem.at[0]
+    )
+    keep_first.start()
+
+    wown[:, 0 : least - half] = kfb_ref[:, half:least]
     rank = b_ref.shape[1]
     width = b_ref.shape[2]
     lows = [dot(g_ref[:, p * width : (p + 1) * width], b_ref[p], 1, 1) for p in range(2)]
@@ -154,16 +198,13 @@
         for t in range(per_shard):
             slot = least + t
             extra = ovf[p, jnp.clip(slot - held, 0, per_shard - 1)]
-            wown[p, slot] = jnp.where(slot < held, kfb_ref[p, slot], extra)
-
-    mine = wown.at[m]
-    for dz in range(1, zs):
-        send(mine, wbuf.at[m, me], wsem_z.at[0, dz], wsem_z.at[1, dz], device(dz=-dz))
-    send(mine, wbuf.at[m, me], wsem_y.at[0, 0], wsem_y.at[1, 0], across_y)
-    send(mine, wbuf.at[m, me], wsem_c.at[0, 0, 0], wsem_c.at[1, 0, 0], sibling)
-    send(wown.at[1 - m], wbuf.at[1 - m, me], wsem_c.at[0, 1, 0], wsem_c.at[1, 1, 0], sibling)
-    keep_own = pltpu.make_async_copy(wown, wbuf.at[:, me], lsem)
-    keep_own.start()
+            wown[p, slot - half] = jnp.where(slot < held, kfb_ref[p, slot], extra)
+
+    w_start(wown, 1)
+    keep_second = pltpu.make_async_copy(
+        wown, wbuf.at[:, me, pl.ds(half, half)], lsem.at[1]
+    )
+    keep_second.start()
 
     low_t = low_ref[...].astype(F32).T.astype(BF16)
     cols = a_ref.shape[0]
@@ -184,25 +225,50 @@
     send(parts.at[1], rc, dsem.at[0, 0], dsem.at[0, 1], sibling)
     down_parts(0)
 
-    def w_from_z(dz):
-        piece = wbuf.at[m, place(dz, 0, 0)]
-        arrived(piece, wsem_z.at[0, dz], wsem_z.at[1, dz], device(dz=dz))
-        send(piece, piece, wsem_y.at[0, dz], wsem_y.at[1, dz], across_y)
-        send(piece, piece, wsem_x.at[0, dz], wsem_x.at[1, dz], across_x)
-        send(piece, piece, wsem_c.at[0, 0, dz], wsem_c.at[1, 0, dz], sibling)
-
-    def w_from_y(dz):
+    orders = [
+        sorted(range(1, zs), key=lambda dz: (dz if zz + dz < zs else zs - dz, zz + dz >= zs))
+        for zz in range(zs)
+    ]
+
+    def nth(i):
+        if i == 0:
+            return 0
+        return sum(jnp.where(z == zz, orders[zz][i - 1], 0) for zz in range(zs))
+
+    def w_from_z(i, c):
+        dz = nth(i)
+        piece = chunk(m, place(dz, 0, 0), c)
+        arrived(piece, wsem_z.at[0, c, 0, dz], wsem_z.at[1, c, 0, dz], device(dz=1))
+        from_above = z + dz < zs
+        step = jnp.where(from_above, zs - 1, 1)
+        at = jnp.where(from_above, lax.rem(dz + 1, zs), dz - 1)
+        further = jnp.where(from_above, z, zs - 1 - z) > 0
+        send(
+            piece,
+            piece,
+            wsem_z.at[0, c, 1, dz],
+            wsem_z.at[1, c, 0, at],
+            (group, place(step, 0, 0)),
+            further,
+        )
+        send(piece, piece, wsem_y.at[0, c, dz], wsem_y.at[1, c, dz], across_y)
+        send(piece, piece, wsem_x.at[0, c, dz], wsem_x.at[1, c, dz], across_x)
+        send(piece, piece, wsem_c.at[0, 0, c, dz], wsem_c.at[1, 0, c, dz], sibling)
+
+    def w_from_y(i, c):
+        dz = nth(i)
         slot = zs + dz
-        piece = wbuf.at[m, place(dz, 1, 0)]
-        arrived(piece, wsem_y.at[0, dz], wsem_y.at[1, dz], across_y)
-        send(piece, piece, wsem_x.at[0, slot], wsem_x.at[1, slot], across_x)
-        send(piece, piece, wsem_c.at[0, 0, slot], wsem_c.at[1, 0, slot], sibling)
-
-    def w_from_x(dz, dy):
+        piece = chunk(m, place(dz, 1, 0), c)
+        arrived(piece, wsem_y.at[0, c, dz], wsem_y.at[1, c, dz], across_y)
+        send(piece, piece, wsem_x.at[0, c, slot], wsem_x.at[1, c, slot], across_x)
+        send(piece, piece, wsem_c.at[0, 0, c, slot], wsem_c.at[1, 0, c, slot], sibling)
+
+    def w_from_x(i, dy, c):
+        dz = nth(i)
         slot = dy * zs + dz
-        piece = wbuf.at[1 - m, place(dz, dy, 0)]
-        arrived(piece, wsem_x.at[0, slot], wsem_x.at[1, slot], across_x)
-        send(piece, piece, wsem_c.at[0, 1, slot], wsem_c.at[1, 1, slot], sibling)
+        piece = chunk(1 - m, place(dz, dy, 0), c)
+        arrived(piece, wsem_x.at[0, c, slot], wsem_x.at[1, c, slot], across_x)
+        send(piece, piece, wsem_c.at[0, 1, c, slot], wsem_c.at[1, 1, c, slot], sibling)
 
     def reduce_y(own, received, landing, ssem, rsem):
         own[0, 1 - y] = own[0, 1 - y] + received[1 - y]
@@ -227,11 +293,17 @@
             total = total + landing[dz]
         return total
 
+    def w_round(i):
+        for c in range(2):
+            w_from_y(i, c)
+            if i + 1 < zs:
+                w_from_z(i + 1, c)
+
     gather_middle(abuf, asem)
     arrived(rc, dsem.at[0, 0], dsem.at[0, 1], sibling)
     reduce_y(parts, rc, ry, dsem.at[1, 0], dsem.at[1, 1])
-    w_from_z(1)
-    w_from_y(0)
+    w_round(0)
+    w_round(1)
     arrived(ry, dsem.at[1, 0], dsem.at[1, 1], across_y)
     reduce_z(parts, ry, rz, dzsem)
     gather_end(abuf, asem)
@@ -258,41 +330,43 @@
         uparts[dk, yy, zz] = ups[owner * rows : (owner + 1) * rows]
     send(uparts.at[1], uc, usem.at[0, 0], usem.at[0, 1], sibling)
 
-    for dz in range(2, zs):
-        w_from_z(dz)
-        w_from_y(dz - 1)
-        if dz == 2:
+    for i in range(2, zs):
+        w_round(i)
+        if i == 2:
             arrived(uc, usem.at[0, 0], usem.at[0, 1], sibling)
             reduce_y(uparts, uc, uy, usem.at[1, 0], usem.at[1, 1])
     arrived(uy, usem.at[1, 0], usem.at[1, 1], across_y)
     reduce_z(uparts, uy, uz, uzsem)
-    w_from_x(1, 0)
-    w_from_x(0, 1)
     down_ref[...] = reduce_end(parts, rz, dzsem)
-    w_from_y(zs - 1)
     ubuf[me] = reduce_end(uparts, uz, uzsem)
     gather_start(ubuf, gsem)
-    for dz in range(2, zs):
-        w_from_x(dz, 0)
-        w_from_x(dz - 1, 1)
-        if dz == 2:
+    for i in range(zs):
+        for c in range(2):
+            w_from_x(i, 1, c)
+            if i + 1 < zs:
+                w_from_x(i + 1, 0, c)
+        if i == 1:
             gather_middle(ubuf, gsem)
-    w_from_x(zs - 1, 1)
     gather_end(ubuf, gsem)
     for p in range(2):
         at = m if p == 0 else 1 - m
-        for dz in range(zs):
-            for dy in range(2):
-                slot = dy * zs + dz
-                arrived(
-                    wbuf.at[at, place(dz, dy, 1)],
-                    wsem_c.at[0, p, slot],
-                    wsem_c.at[1, p, slot],
-                    sibling,
-                )
-    for copy in sends:
-        copy.wait_send()
-    keep_own.wait()
+        for c in range(2):
+            for dz in range(zs):
+                for dy in range(2):
+                    slot = dy * zs + dz
+                    arrived(
+                        chunk(at, place(dz, dy, 1), c),
+                        wsem_c.at[0, p, c, slot],
+                        wsem_c.at[1, p, c, slot],
+                        sibling,
+                    )
+    for copy, when in sends:
+        if when is None:
+            copy.wait_send()
+        else:
+            pl.when(when)(copy.wait_send)
+    keep_first.wait()
+    keep_second.wait()
 
 
 def rows_kernel(row_blocks, table_ref, w_ref, a_ref, g_ref, low_ref, out_ref, dense):
@@ -361,7 +435,7 @@
         in_specs=[smem, vmem, vmem, vmem, vmem, vmem],
         out_specs=(hbm, vmem, vmem, vmem, vmem),
         scratch_shapes=[
-            pltpu.VMEM((2, full, block, block), BF16),
+            pltpu.VMEM((2, full // 2, block, block), BF16),
             pltpu.VMEM((2, per_shard, block, block), BF16),
             pltpu.VMEM((2, 2, zs, 2 * rank, cols), F32),
             pltpu.VMEM((2, zs, 2 * rank, cols), F32),
@@ -372,17 +446,17 @@
             pltpu.VMEM((zs, rows, width), F32),
             pltpu.VMEM((zs, rows, width), F32),
             dma((3, 2, 2 * zs)),
-            dma((2, zs)),
-            dma((2, zs)),
-            dma((2, 2 * zs)),
+            dma((2, 2, 2, zs)),
+            dma((2, 2, zs)),
             dma((2, 2, 2 * zs)),
+            dma((2, 2, 2, 2 * zs)),
             dma((2,)),
             dma((2, 2)),
             dma((2, zs)),
             dma((2, 2)),
             dma((2, zs)),
             dma((3, 2, 2 * zs)),
-            dma(()),
+            dma((2,)),
         ],
         compiler_params=pltpu.CompilerParams(
             collective_id=0, has_side_effects=True, vmem_limit_bytes=48 * 2**20

time: 183 us -> 172 us (0.940)
  the two profiles are of different devices: /device:TPU:13 before, /device:TPU:1 now
where the time goes in v2:
time: 172 us; the launch traced here: 171 us
  Pallas kernels  161 us (94%)
  local copies, waits for them, and re-layouts  7.71 us (4%)
    pallas_call x1, Pallas kernels, on_device(): pl.pallas_call(functools.partial(exchange_kernel, n, scale), out_shape=(j...  136 us
    pallas_call x1, Pallas kernels, on_device(): pl.pallas_call(functools.partial(rows_kernel, row_blocks), out_shape=jax....  25.4 us
    unnamed x11, local copies, waits for them, and re-layouts  6.91 us

profile of v2, /device:TPU:1, one launch (start us, length us, event | category | flops | bytes accessed | tf_op | source)
XLA Modules:
  0.0 170.9 jit_solution(7452087083756110426)
XLA Ops:
  0.7 0.7 reduce_sum.10
  1.4 0.1 reduce_sum.14
  1.5 0.1 reduce_sum.18
  1.6 0.2 dynamic-slice_reduce_fusion.count_ref
  1.8 0.1 add.54
  1.8 0.1 add.55
  1.9 0.1 add.49
  2.0 0.1 add.50
  2.1 0.8 copy.18
  2.9 0.1 reshape.67
  3.0 0.1 reshape.68
  3.0 0.4 reduce_window_sum.13
  3.4 0.1 reduce_window_sum.14
  3.5 0.0 copy-start
  3.5 1.3 copy-done
  4.8 0.0 copy-start.1
  4.8 1.3 copy-done.1
  6.2 0.0 copy-start.2
  6.2 0.9 copy-done.2
  7.1 0.0 copy-start.3
  7.1 0.9 copy-done.3
  8.0 135.8 %exchange.1 = (bf16[2,16,16,128,128]{4,3,2,1,0:T(8,128)(2,1)}, bf16[16,512,128]{2,1,0:T(8,128)(2,1)S(1)}, bf16[320,128]{1,0:T(8,128)(2,1)S(1)}, f32[128,512]{1,0:T(8,128)S(1)}, f32[16,8,1024]{2,1,0:T(8,128)S(1)}) custom-call(s32[2]{0:T(128)S(1)} %dynamic-slice_reduce_fusion.count_ref, bf16[320,8192]{1,0:T(8,128)(2,1)} %x_ref.1, ...), custom_call_target="tpu_custom_call" | custom-call | tf_op jit(solution)/shard_map/exchange/pallas_call | solution.py:426
  143.9 25.4 %rows.1 = bf16[320,8192]{1,0:T(8,128)(2,1)} custom-call(s32[1024]{0:T(1024)S(1)} %select_select_fusion.table_ref, bf16[2,2,8,16,128,128]{5,4,3,2,1,0:T(8,128)(2,1)} %bitcast.7, bf16[8192,128]{1,0:T(8,128)(2,1)S(1)} %bitcast.4, bf16[320,2048]{1,0:T(8,128)(2,1)S(1)} %copy-done, bf16[320,128]{1,0:T(8,128)(2,1)S(1)} %get-tuple-element.10.low_ref), custom_call_target="tpu_custom_call" | custom-call | tf_op jit(solution)/shard_map/rows/pallas_call | solution.py:475
  169.3 0.8 copy.20
  170.1 0.8 copy.22
  (4 shorter events, 0.0 us)
Async XLA Ops:
  3.5 1.3 copy-start
  4.8 1.3 copy-start.1
  6.2 0.9 copy-start.2
  7.1 0.9 copy-start.3

commit v3 on v2

--- a/solution.py
+++ b/solution.py
@@ -21,7 +21,7 @@
     n,
     scale,
     count_ref,
-    x_ref,
+    x_hbm,
     g_ref,
     kfb_ref,
     a_ref,
@@ -31,6 +31,7 @@
     low_ref,
     down_ref,
     ubuf,
+    x_ref,
     wown,
     ovf,
     parts,
@@ -53,7 +54,10 @@
     uzsem,
     gsem,
     lsem,
+    xsem,
 ):
+    load = pltpu.make_async_copy(x_hbm, x_ref, xsem)
+    load.start()
     zs = n // 4
     group = lax.axis_index("groups")
     me = lax.axis_index("fsdp")
@@ -221,6 +225,7 @@
 
             lax.fori_loop(0, zs, body, 0)
 
+    load.wait()
     down_parts(1)
     send(parts.at[1], rc, dsem.at[0, 0], dsem.at[0, 1], sibling)
     down_parts(0)
@@ -369,24 +374,24 @@
     keep_second.wait()
 
 
-def rows_kernel(row_blocks, table_ref, w_ref, a_ref, g_ref, low_ref, out_ref, dense):
+def rows_kernel(row_blocks, table_ref, w_ref, a_ref, g_ref, low_ref, out_ref):
     shard = pl.program_id(1) * pl.num_programs(0) + pl.program_id(0)
     full = w_ref.shape[3]
     block = w_ref.shape[-1]
     per_shard = out_ref.shape[1] // block
     col_blocks = g_ref.shape[1] // (2 * block)
     zero = jnp.zeros((block, block), BF16)
-    for m in range(2):
-        for r in range(per_shard):
-            for c in range(col_blocks):
-                code = table_ref[(m * row_blocks + shard * per_shard + r) * col_blocks + c]
-                at = jnp.maximum(code, 0)
-                taken = w_ref[m, at // full, 0, lax.rem(at, full)]
-                col = (m * col_blocks + c) * block
-                dense[r * block : (r + 1) * block, col : col + block] = jnp.where(
-                    code >= 0, taken, zero
-                )
-    total = dot(g_ref[...], dense[...], 1, 1)
+
+    def taken(m, r, c):
+        code = table_ref[(m * row_blocks + shard * per_shard + r) * col_blocks + c]
+        at = jnp.maximum(code, 0)
+        return jnp.where(code >= 0, w_ref[m, at // full, 0, lax.rem(at, full)], zero)
+
+    rows = [
+        jnp.concatenate([taken(m, r, c) for m in range(2) for c in range(col_blocks)], axis=1)
+        for r in range(per_shard)
+    ]
+    total = dot(g_ref[...], jnp.concatenate(rows, axis=0), 1, 1)
     total = total + adapter_scale * dot(low_ref[...], a_ref[...], 1, 1)
     out_ref[...] = total.astype(BF16)
 
@@ -432,9 +437,10 @@
             jax.ShapeDtypeStruct((2 * rank, cols), F32),
             jax.ShapeDtypeStruct((n, rows, width), F32),
         ),
-        in_specs=[smem, vmem, vmem, vmem, vmem, vmem],
+        in_specs=[smem, hbm, vmem, vmem, vmem, vmem],
         out_specs=(hbm, vmem, vmem, vmem, vmem),
         scratch_shapes=[
+            pltpu.VMEM((tokens, model_width), BF16),
             pltpu.VMEM((2, full // 2, block, block), BF16),
             pltpu.VMEM((2, per_shard, block, block), BF16),
             pltpu.VMEM((2, 2, zs, 2 * rank, cols), F32),
@@ -457,9 +463,10 @@
             dma((2, zs)),
             dma((3, 2, 2 * zs)),
             dma((2,)),
+            dma(()),
         ],
         compiler_params=pltpu.CompilerParams(
-            collective_id=0, has_side_effects=True, vmem_limit_bytes=48 * 2**20
+            collective_id=0, has_side_effects=True, vmem_limit_bytes=56 * 2**20
         ),
         name="exchange",
     )(
@@ -487,7 +494,6 @@
                 pl.BlockSpec((tokens, 2 * rank), lambda p, h, t: (0, 0)),
             ],
             out_specs=pl.BlockSpec((tokens, shard_cols), lambda p, h, t: (0, h * (n // 2) + p)),
-            scratch_shapes=[pltpu.VMEM((shard_cols, 2 * width), BF16)],
         ),
         compiler_params=pltpu.CompilerParams(vmem_limit_bytes=40 * 2**20),
         name="rows",

time: 172 us -> 169 us (0.983)
    unnamed x11 -> x13, local copies, waits for them, and re-layouts: 6.91 us -> 4.9 us
    pallas_call x1, Pallas kernels: 25.4 us -> 23.5 us  [on_device(): pl.pallas_call(functools.partial(rows_kernel, row_blocks), out_shape=jax....]
where the time goes in v3:
time: 169 us; the launch traced here: 168 us
  Pallas kernels  160 us (95%)
  local copies, waits for them, and re-layouts  6.23 us (4%)
    pallas_call x1, Pallas kernels, on_device(): pl.pallas_call(functools.partial(exchange_kernel, n, scale), out_shape=(j...  137 us
    pallas_call x1, Pallas kernels, on_device(): pl.pallas_call(functools.partial(rows_kernel, row_blocks), out_shape=jax....  23.5 us
    unnamed x13, local copies, waits for them, and re-layouts  4.9 us

profile of v3, /device:TPU:1, one launch (start us, length us, event | category | flops | bytes accessed | tf_op | source)
XLA Modules:
  0.0 168.5 jit_solution(7781531658684214986)
XLA Ops:
  0.6 0.0 copy-start
  0.7 0.8 reduce_sum.10
  1.5 0.1 reduce_sum.14
  1.6 0.1 reduce_sum.18
  1.7 0.7 dynamic-slice_reduce_fusion.count_ref
  2.4 0.1 add.54
  2.5 0.1 add.55
  2.5 0.1 add.49
  2.6 0.1 add.50
  2.7 0.8 copy.18
  3.5 0.1 reshape.67
  3.6 0.1 reshape.68
  3.7 0.4 reduce_window_sum.13
  4.1 0.1 reduce_window_sum.14
  4.1 136.7 %exchange.1 = (bf16[2,16,16,128,128]{4,3,2,1,0:T(8,128)(2,1)}, bf16[16,512,128]{2,1,0:T(8,128)(2,1)}, bf16[320,128]{1,0:T(8,128)(2,1)}, f32[128,512]{1,0:T(8,128)}, f32[16,8,1024]{2,1,0:T(8,128)}) custom-call(s32[2]{0:T(128)} %dynamic-slice_reduce_fusion.count_ref, bf16[320,8192]{1,0:T(8,128)(2,1)} %x_hbm.1, bf16[320,2048]{1,0:T(8,128)(2,1)} %g_ref.3, ...), custom_call_target="tpu_custom_call" | custom-call | tf_op jit(solution)/shard_map/exchange/pallas_call | solution.py:431
  140.9 0.0 copy-done
  140.9 0.0 copy-start.1
  140.9 1.6 copy-done.1
  142.5 0.0 copy-start.2
  142.5 0.9 copy-done.2
  143.4 0.0 copy-start.4
  143.4 0.0 copy-start.3
  143.4 23.5 %rows.1 = bf16[320,8192]{1,0:T(8,128)(2,1)} custom-call(s32[1024]{0:T(1024)S(1)} %select_select_fusion.table_ref, bf16[2,2,8,16,128,128]{5,4,3,2,1,0:T(8,128)(2,1)} %bitcast.5, bf16[8192,128]{1,0:T(8,128)(2,1)S(1)} %bitcast.4, bf16[320,2048]{1,0:T(8,128)(2,1)S(1)} %copy-done, bf16[320,128]{1,0:T(8,128)(2,1)S(1)} %copy-done.2), custom_call_target="tpu_custom_call" | custom-call | tf_op jit(solution)/shard_map/rows/pallas_call | solution.py:482
  166.8 0.0 copy-done.4
  166.8 0.8 copy.20
  167.7 0.0 copy-done.3
  167.7 0.8 copy.22
  (4 shorter events, 0.0 us)
Async XLA Ops:
  0.6 140.3 %copy-start = (bf16[320,2048]{1,0:T(8,128)(2,1)S(1)}, bf16[320,2048]{1,0:T(8,128)(2,1)}, u32[]{:S(2)}) copy-start(bf16[320,2048]{1,0:T(8,128)(2,1)} %g_ref.3) | copy-start | bytes 3932164
  140.9 1.6 copy-start.1
  142.5 0.9 copy-start.2
  143.4 23.5 %copy-start.4 = (f32[128,512]{1,0:T(8,128)S(1)}, f32[128,512]{1,0:T(8,128)}, u32[]{:S(2)}) copy-start(f32[128,512]{1,0:T(8,128)} %get-tuple-element.11) | copy-start | bytes 786436
  143.4 24.3 %copy-start.3 = (f32[16,8,1024]{2,1,0:T(8,128)S(1)}, f32[16,8,1024]{2,1,0:T(8,128)}, u32[]{:S(2)}) copy-start(f32[16,8,1024]{2,1,0:T(8,128)} %get-tuple-element.12) | copy-start | bytes 1572868
